TPU v7x, 32 devices: a whole 2x2x4 slice. The times are simulated.
32 devices in a mesh: ja: 2 (over x), ka: 4 (over z), ia: 4 (over y, core).
Axes of the slice: x: 2, y: 2, z: 4, core: 2. Of those that a mesh axis runs over, the one named last changes fastest.
Arguments:
- tensor: float32 [48, 1024, 2048], P('ia', 'ja', 'ka'), may hold values from -6 to 6
- factor_b: float32 [1024, 256], P(('ja', 'ka', 'ia')), may hold values from -0.9 to 0.9, as said below
- factor_c: float32 [2048, 256], P(('ka', 'ja', 'ia')), may hold values from -0.9 to 0.9, as said below
Outputs:
- new_factor: float32 [48, 256], P('ia')
Inputs may be any that keep to these rules, and one draw needn't show every extreme that they name: `factor_b`: real entries of the factor. `factor_c`: real entries of the factor.
All inputs are finite; a program needn't handle non-finite values.
Results may differ from a plain program's by a relative error of at most 0.000086.
Values sent between devices are 32-bit elements; how exact they have to be, the bound alone decides.
A program may use at most 64 MiB of HBM per device.

v0:
```python
import jax
import jax.numpy as jnp
from jax import lax
from jax.sharding import PartitionSpec as P

exact_mode = lax.Precision.HIGHEST


def gram_of(matrix):
    return jnp.dot(matrix.T, matrix, precision=exact_mode, preferred_element_type=jnp.float32)


def shards(tensor, factor_b, factor_c):
    slab_rows, mode_two, mode_three = tensor.shape
    width = factor_b.shape[1]
    gram_b, gram_c = lax.psum((gram_of(factor_b), gram_of(factor_c)), ("ja", "ka", "ia"))
    upper_b = jnp.linalg.cholesky(gram_b).T
    upper_c = jnp.linalg.cholesky(gram_c).T
    unfolded = tensor.reshape(slab_rows * mode_two, mode_three)
    empty_gram = jnp.zeros((width, width), jnp.float32)
    section_sum = jnp.dot(
        unfolded,
        lax.all_gather(factor_c, ("ja", "ia"), axis=0, tiled=True),
        precision=exact_mode,
        preferred_element_type=jnp.float32,
    )
    section_three = section_sum.reshape(slab_rows, mode_two, width)
    partial_sum = jnp.sum(
        section_three * lax.all_gather(factor_b, ("ka", "ia"), axis=0, tiled=True)[None, :, :],
        axis=1,
    )
    partial_sum, block_gram_b = (partial_sum, empty_gram)
    product = lax.psum(partial_sum, ("ja", "ka"))
    normal = gram_of(upper_b) * gram_of(upper_c)
    lower_factor = jnp.linalg.cholesky(normal)
    halfway = lax.linalg.triangular_solve(lower_factor, product.T, left_side=True, lower=True)
    solved = lax.linalg.triangular_solve(
        lower_factor, halfway, left_side=True, lower=True, transpose_a=True
    )
    return solved.T


def solution(mesh):
    return jax.shard_map(
        shards,
        mesh=mesh,
        in_specs=(P("ia", "ja", "ka"), P(("ja", "ka", "ia"), None), P(("ka", "ja", "ia"), None)),
        out_specs=P("ia", None),
        check_vma=False,
    )
```

profile of v0, /device:TPU:0, one launch (start us, length us, event | category | flops | bytes accessed | tf_op | source)
XLA Modules:
  0.0 291.1 jit_solution(8396400125654951190)
XLA Ops:
  6.5 2.0 fusion.44
  8.5 2.0 fusion.45
  10.6 25.1 %all_gather.7 = f32[512,256]{1,0:T(8,128)S(1)} all-gather(f32[32,256]{1,0:T(8,128)} %param.5), channel_id=1, replica_groups=mesh['ja'=2,'ka'=4,'ia'=4] {'ka','ia'}, dimensions={0}, use_global_device_ids=true | all-gather | bytes 557056 | tf_op jit(solution)/shard_map/all_gather | solution.py:29
  35.6 9.8 %all_gather.6 = f32[512,256]{1,0:T(8,128)S(1)} all-gather(f32[64,256]{1,0:T(8,128)} %param.6), channel_id=1, replica_groups=mesh['ja'=2,'ka'=4,'ia'=4] {'ja','ia'}, dimensions={0}, use_global_device_ids=true | all-gather | bytes 589824 | tf_op jit(solution)/shard_map/all_gather | solution.py:23
  45.5 13.2 %multiply_reduce_fusion = f32[12,256]{1,0:T(8,128)S(1)} fusion(f32[512,256]{1,0:T(8,128)S(1)} %all_gather.7, f32[12,512,512]{2,1,0:T(8,128)} %param.4, f32[512,256]{1,0:T(8,128)S(1)} %all_gather.6), kind=kOutput, calls=%fused_computation.2 | convolution fusion | flops 9666819072 | bytes 13643776 | tf_op jit(solution)/shard_map/dot_general | solution.py:21
  58.7 33.4 %psum.23 = f32[256,12]{0,1:T(8,128)S(1)} all-reduce(f32[256,12]{0,1:T(8,128)S(1)} %bitcast.73), channel_id=1, replica_groups=mesh['ja'=2,'ka'=4,'ia'=4] {'ja','ka'}, use_global_device_ids=true, to_apply=%region_7.9 | all-reduce | flops 3072 | bytes 24576 | tf_op jit(solution)/shard_map/psum | solution.py:33
  92.1 51.8 %all-reduce.4.cloned.1.call-done = (f32[256,256]{0,1:T(8,128)}, f32[256,256]{0,1:T(8,128)}) async-done(((f32[256,256]{0,1:T(8,128)}, f32[256,256]{0,1:T(8,128)}), (f32[256,256]{0,1:T(8,128)}, f32[256,256]{0,1:T(8,128)})) %all-reduce.4.cloned.1.call-update) | async-done | bytes 524304 | tf_op jit(solution)/shard_map/psum | solution.py:16
  143.9 1.1 copy.5
  145.0 1.1 copy.7
  146.1 1.1 fusion.2
  147.2 11.7 %cholesky.206 = f32[128,128]{1,0:T(8,128)S(1)} custom-call(f32[128,128]{1,0:T(8,128)S(1)} %cholesky.273), custom_call_target="Cholesky" | custom-call | tf_op jit(solution)/shard_map/jit(cholesky)/cholesky | solution.py:18
  158.9 11.7 %cholesky.172 = f32[128,128]{1,0:T(8,128)S(1)} custom-call(f32[128,128]{1,0:T(8,128)S(1)} %cholesky.270), custom_call_target="Cholesky" | custom-call | tf_op jit(solution)/shard_map/jit(cholesky)/cholesky | solution.py:17
  170.8 0.7 compare_reduce_fusion.5
  171.5 9.8 %custom-call.16 = f32[1,128,128]{1,2,0:T(8,128)S(1)} custom-call(f32[1,128,128]{2,1,0:T(8,128)S(1)} %get-tuple-element.37), custom_call_target="InvertDiagBlocksLowerTriangular" | custom-call | tf_op jit(solution)/shard_map/jit(cholesky)/cholesky | solution.py:17
  181.3 0.7 compare_reduce_fusion.3
  182.0 10.0 %custom-call.17 = f32[1,128,128]{1,2,0:T(8,128)S(1)} custom-call(f32[1,128,128]{2,1,0:T(8,128)S(1)} %get-tuple-element.33), custom_call_target="InvertDiagBlocksLowerTriangular" | custom-call | tf_op jit(solution)/shard_map/jit(cholesky)/cholesky | solution.py:18
  191.9 0.2 constant_dynamic-update-slice_fusion.3
  192.2 0.3 convolution_subtract_fusion.1
  192.4 11.7 %cholesky.223 = f32[128,128]{1,0:T(8,128)S(1)} custom-call(f32[128,128]{1,0:T(8,128)S(1)} %convolution_subtract_fusion.1), custom_call_target="Cholesky" | custom-call | tf_op jit(solution)/shard_map/jit(cholesky)/cholesky | solution.py:18
  204.2 0.7 compare_reduce_fusion.2
  204.9 0.2 constant_dynamic-update-slice_fusion.5
  205.1 0.3 convolution_subtract_fusion.2
  205.4 11.7 %cholesky.189 = f32[128,128]{1,0:T(8,128)S(1)} custom-call(f32[128,128]{1,0:T(8,128)S(1)} %convolution_subtract_fusion.2), custom_call_target="Cholesky" | custom-call | tf_op jit(solution)/shard_map/jit(cholesky)/cholesky | solution.py:17
  217.1 0.6 compare_reduce_fusion.4
  220.3 0.4 fusion.6
  220.7 0.4 convolution_multiply_fusion
  221.1 0.1 copy.10
  221.3 11.9 %cholesky.240 = f32[128,128]{1,0:T(8,128)S(1)} custom-call(f32[128,128]{1,0:T(8,128)S(1)} %cholesky.276), custom_call_target="Cholesky" | custom-call | tf_op jit(solution)/shard_map/jit(cholesky)/cholesky | solution.py:35
  233.3 0.7 compare_reduce_fusion.1
  234.0 9.8 %custom-call.18 = f32[1,128,128]{1,2,0:T(8,128)S(1)} custom-call(f32[1,128,128]{2,1,0:T(8,128)S(1)} %get-tuple-element.29), custom_call_target="InvertDiagBlocksLowerTriangular" | custom-call | tf_op jit(solution)/shard_map/jit(cholesky)/cholesky | solution.py:35
  243.9 0.2 constant_dynamic-update-slice_fusion.1
  244.1 0.3 convolution_subtract_fusion
  244.3 11.7 %cholesky.257 = f32[128,128]{1,0:T(8,128)S(1)} custom-call(f32[128,128]{1,0:T(8,128)S(1)} %convolution_subtract_fusion), custom_call_target="Cholesky" | custom-call | tf_op jit(solution)/shard_map/jit(cholesky)/cholesky | solution.py:35
  256.1 0.6 compare_reduce_fusion
  258.0 0.1 triangular_solve.63
  258.1 4.1 %while.1 = (s32[]{:T(128)}, f32[256,256]{1,0:T(8,128)S(1)}, s32[2,2]{1,0:T(2,128)S(1)}, f32[2,128,128]{2,1,0:T(8,128)S(1)}, s32[]{:T(128)}) while((s32[]{:T(128)}, f32[256,256]{1,0:T(8,128)S(1)}, s32[2,2]{1,0:T(2,128)S(1)}, f32[2,128,128]{2,1,0:T(8,128)S(1)}, s32[]{:T(128)}) %tuple.30), condition=%wide.while_cond, body=%wide.while_body.sunk | while | flops 2 | bytes 131189 | solution.py:37
  258.1 0.7 fusion.63
  258.8 1.3 bitcast_dynamic-update-slice_fusion.2
  260.1 0.7 fusion.63
  260.8 1.3 bitcast_dynamic-update-slice_fusion.2
  262.1 19.7 %custom-call.13 = f32[2,128,128]{1,2,0:T(8,128)S(1)} custom-call(f32[2,128,128]{2,1,0:T(8,128)S(1)} %get-tuple-element.13), custom_call_target="InvertDiagBlocksLowerTriangular" | custom-call | tf_op jit(solution)/shard_map/triangular_solve | solution.py:37
  281.8 0.2 fusion.33
  282.0 0.2 convolution_subtract_fusion.4
  282.2 0.3 fusion.35
  282.5 0.2 fusion.34
  282.7 0.2 convolution_subtract_fusion.3
  282.9 0.2 fusion.32
  283.1 0.7 maximum_bitcast_fusion
  (20 shorter events, 0.4 us)
Async XLA Ops:
  6.5 137.4 %all-reduce.4.cloned.1.call-start = ((), (), s32[]{:S(2)}) async-start(), calls=%async_computation | async-start | bytes 1048576 | tf_op jit(solution)/shard_map/psum | solution.py:16
Sparse Core Ops, SparseCore 0:
  12.8 131.0 all-reduce.3
where the time goes:
time: 297 us; the launch traced here: 291 us
  other arithmetic  126 us (42%)
  blocking collectives  68.3 us (23%)
  waiting for transfers between devices  51.8 us (17%)
  matrix products  20.8 us (7%)
  between operations  17.8 us (6%)
  local copies, waits for them, and re-layouts  6.45 us (2%)
    psum x1, waiting for transfers between devices, shards(): lax.psum((gram_of(factor_b), gram_of(factor_c)), ('ja', 'ka', 'ia'))  51.8 us
    another operation x7, other arithmetic, shards(): lower_factor = jnp.linalg.cholesky(normal)  34.9 us
    another operation x7, other arithmetic, shards(): upper_c = jnp.linalg.cholesky(gram_c).T  34.9 us
    another operation x7, other arithmetic, shards(): upper_b = jnp.linalg.cholesky(gram_b).T  34.7 us
    psum x1, blocking collectives, shards(): product = lax.psum(partial_sum, ('ja', 'ka'))  33.4 us
    all_gather x1, blocking collectives, shards(): lax.all_gather(factor_b, ('ka', 'ia'), axis=0, tiled=True)[None, :, :]  25.1 us
    another operation x3, other arithmetic, shards(): lax.linalg.triangular_solve(lower_factor, halfway, left_side=True, lower=...  19.7 us
    dot_general x1, matrix products, shards(): jnp.dot(unfolded, lax.all_gather(factor_c, ('ja', 'ia'), axis=0, tiled=Tr...  13.2 us
  transfers between devices with their start and end apart: 1, of which 1 were waited for; matrix products, arithmetic and copies ran while one was open for 5% of the time, Pallas kernels for 0%

commit v1 on v0

v1 whole, which is shorter than its diff:
```python
import functools

import jax
import jax.numpy as jnp
from jax import lax
from jax.experimental import pallas as pl
from jax.experimental.pallas import tpu as pltpu
from jax.sharding import PartitionSpec as P

exact_mode = lax.Precision.HIGHEST
tile_rows = 8


def bits_of(count):
    found, bit = [], count // 2
    while bit >= 1:
        found.append(bit)
        bit //= 2
    return found


def flip(index, bit):
    return index + bit * (1 - 2 * ((index // bit) % 2))


def flip_mask(index, mask):
    bit = 1
    while bit <= mask:
        if mask & bit:
            index = flip(index, bit)
        bit *= 2
    return index


def exact_dot(a, b, dims):
    return lax.dot_general(
        a, b, (dims, ((), ())), precision=exact_mode, preferred_element_type=jnp.float32
    )


class Gather:
    def __init__(self, buffer, send_sems, recv_sems, position, links):
        self.buffer, self.send_sems, self.recv_sems = buffer, send_sems, recv_sems
        self.position, self.links = position, links
        self.sends = []

    def forward(self, mask):
        low = mask & -mask
        chunk = flip_mask(self.position, mask)
        for bit, device in self.links:
            if mask == 0 or bit < low:
                copy = pltpu.make_async_remote_copy(
                    src_ref=self.buffer.at[chunk],
                    dst_ref=self.buffer.at[chunk],
                    send_sem=self.send_sems.at[mask | bit],
                    recv_sem=self.recv_sems.at[mask | bit],
                    device_id=device,
                    device_id_type=pl.DeviceIdType.MESH,
                )
                copy.start()
                self.sends.append(copy)

    def arrive(self, mask):
        low = mask & -mask
        chunk = flip_mask(self.position, mask)
        device = [d for bit, d in self.links if bit == low][0]
        pltpu.make_async_remote_copy(
            src_ref=self.buffer.at[chunk],
            dst_ref=self.buffer.at[chunk],
            send_sem=self.send_sems.at[mask],
            recv_sem=self.recv_sems.at[mask],
            device_id=device,
            device_id_type=pl.DeviceIdType.MESH,
        ).wait_recv()

    def masks(self):
        count = 2 ** len(self.links)
        return sorted(range(1, count), key=lambda m: (bin(m).count("1"), -m))

    def finish(self):
        for copy in self.sends:
            copy.wait_send()


def exchange_kernel(
    names,
    sizes,
    tensor_ref,
    b_ref,
    c_ref,
    normal_ref,
    product_ref,
    t_buf,
    b_buf,
    c_buf,
    n_buf,
    gram_b,
    gram_c,
    b_in,
    c_in,
    p_in,
    c_high,
    c_low,
    b_flat,
    p_buf,
    t_sem,
    b_send,
    b_recv,
    c_send,
    c_recv,
    n_send,
    n_recv,
    gb_sem,
    gc_sem,
    p_sem,
):
    slab_rows = tensor_ref.shape[0]
    width = b_ref.shape[1]
    at = {name: lax.axis_index(name) for name in names}

    def partner(name, bit):
        return tuple(flip(at[n], bit) if n == name else at[n] for n in names)

    def fetch(i):
        return pltpu.make_async_copy(tensor_ref.at[i], t_buf.at[i], t_sem.at[i])

    for i in range(slab_rows):
        fetch(i).start()

    partners = [partner(n, bit) for n in names for bit in bits_of(sizes[n])]
    barrier = pltpu.get_barrier_semaphore()
    for device in partners:
        pl.semaphore_signal(barrier, inc=1, device_id=device, device_id_type=pl.DeviceIdType.MESH)

    ia_links = [(bit, partner("ia", bit)) for bit in bits_of(sizes["ia"])]
    c_links = [(bit * sizes["ia"], partner("ja", bit)) for bit in bits_of(sizes["ja"])] + ia_links
    b_links = [(bit * sizes["ia"], partner("ka", bit)) for bit in bits_of(sizes["ka"])] + ia_links
    c_at = at["ja"] * sizes["ia"] + at["ia"]
    b_at = at["ka"] * sizes["ia"] + at["ia"]
    c_buf[c_at] = c_ref[...]
    b_buf[b_at] = b_ref[...]
    pl.semaphore_wait(barrier, len(partners))

    c_all = Gather(c_buf, c_send, c_recv, c_at, c_links)
    b_all = Gather(b_buf, b_send, b_recv, b_at, b_links)
    c_all.forward(0)
    b_all.forward(0)
    for mask in c_all.masks():
        c_all.arrive(mask)
        c_all.forward(mask)

    deep = c_buf.shape[0] * c_buf.shape[1]
    whole_c = c_buf[...].reshape(deep, width)
    high = whole_c.astype(jnp.bfloat16)
    c_high[...] = high
    c_low[...] = (whole_c - high.astype(jnp.float32)).astype(jnp.bfloat16)
    gram_c[...] = exact_dot(whole_c, whole_c, ((0,), (0,)))

    slab = width // sizes["ia"]
    rows = pl.ds(pl.multiple_of(at["ia"] * slab, slab), slab)

    def stage(buffer, inbox, sems, step, device):
        return pltpu.make_async_remote_copy(
            src_ref=buffer,
            dst_ref=inbox.at[step],
            send_sem=sems.at[0, step],
            recv_sem=sems.at[1, step],
            device_id=device,
            device_id_type=pl.DeviceIdType.MESH,
        )

    ka_partners = [partner("ka", bit) for bit in bits_of(sizes["ka"])]
    ja_partners = [partner("ja", bit) for bit in bits_of(sizes["ja"])]
    c_steps = [stage(gram_c.at[rows], c_in, gc_sem, s, d) for s, d in enumerate(ka_partners)]
    b_steps = [stage(gram_b.at[rows], b_in, gb_sem, s, d) for s, d in enumerate(ja_partners)]
    c_steps[0].start()

    for mask in b_all.masks():
        b_all.arrive(mask)
        b_all.forward(mask)
    whole_b = b_buf[...].reshape(b_buf.shape[0] * b_buf.shape[1], width)
    b_flat[...] = whole_b
    gram_b[...] = exact_dot(whole_b, whole_b, ((0,), (0,)))
    b_steps[0].start()

    def rows_of_product(first, last):
        def one(i, carry):
            fetch(i).wait()
            block = t_buf[i]
            block_high = block.astype(jnp.bfloat16)
            block_low = (block - block_high.astype(jnp.float32)).astype(jnp.bfloat16)
            dims = ((1,), (0,))

            def pass_of(left, right):
                return lax.dot_general(
                    left, right, (dims, ((), ())), preferred_element_type=jnp.float32
                )

            section = (
                pass_of(block_low, c_high[...])
                + pass_of(block_high, c_low[...])
                + pass_of(block_high, c_high[...])
            )
            p_buf[pl.ds(i, 1), :] = jnp.sum(section * b_flat[...], axis=0, keepdims=True)
            return carry

        lax.fori_loop(first, last, one, 0)

    pending = [("c", s) for s in range(len(c_steps))] + [("b", s) for s in range(len(b_steps))]
    parts = len(pending) + 1
    cuts = [slab_rows * p // parts for p in range(parts + 1)]
    for part, (kind, step) in enumerate(pending):
        rows_of_product(cuts[part], cuts[part + 1])
        steps, buffer, inbox = (
            (c_steps, gram_c, c_in) if kind == "c" else (b_steps, gram_b, b_in)
        )
        steps[step].wait()
        buffer[rows, :] += inbox[step]
        if step + 1 < len(steps):
            steps[step + 1].start()

    n_buf[at["ia"]] = gram_b[rows, :] * gram_c[rows, :]
    n_all = Gather(n_buf, n_send, n_recv, at["ia"], ia_links)
    n_all.forward(0)
    rows_of_product(cuts[parts - 1], cuts[parts])
    p_steps = [stage(p_buf, p_in, p_sem, s, d) for s, d in enumerate(ja_partners + ka_partners)]
    p_steps[0].start()
    for mask in n_all.masks():
        n_all.arrive(mask)
        n_all.forward(mask)
    normal_ref[...] = n_buf[...].reshape(width, width)
    for step, copy in enumerate(p_steps):
        copy.wait()
        p_buf[...] += p_in[step]
        if step + 1 < len(p_steps):
            p_steps[step + 1].start()
    product_ref[...] = p_buf[...]
    n_all.finish()
    b_all.finish()
    c_all.finish()


def inverse_of(matrix):
    size = matrix.shape[0]
    count = size // tile_rows
    blocks = [matrix[tile_rows * i : tile_rows * (i + 1), :] for i in range(count)]
    lane = lax.broadcasted_iota(jnp.int32, (tile_rows, size), 1)
    row = lax.broadcasted_iota(jnp.int32, (tile_rows, size), 0)
    full = (tile_rows, size)
    for b in range(count):
        start = tile_rows * b
        inside = (lane >= start) & (lane < start + tile_rows)
        own = [
            jnp.broadcast_to(blocks[b][:, start + j : start + j + 1], full)
            for j in range(tile_rows)
        ]
        panel = jnp.where(inside, jnp.where(lane - start == row, 1.0, 0.0), blocks[b])
        for j in range(tile_rows):
            scale = 1.0 / jnp.broadcast_to(own[j][j : j + 1, :], full)
            here = row == j
            factor = jnp.where(here, 0.0, own[j])
            for c in range(j + 1, tile_rows):
                line = jnp.broadcast_to(own[c][j : j + 1, :], full) * scale
                own[c] = jnp.where(here, line, own[c] - factor * line)
            line = jnp.broadcast_to(panel[j : j + 1, :], full) * scale
            panel = jnp.where(here, line, panel - factor * line)
        lines = [jnp.broadcast_to(panel[j : j + 1, :], full) for j in range(tile_rows)]
        for i in range(count):
            if i == b:
                continue
            new = jnp.where(inside, 0.0, blocks[i])
            for j in range(tile_rows):
                new = new - jnp.broadcast_to(blocks[i][:, start + j : start + j + 1], full) * lines[j]
            blocks[i] = new
        blocks[b] = panel
    return jnp.concatenate(blocks, axis=0)


def solve_kernel(normal_ref, product_ref, out_ref):
    half = normal_ref.shape[0] // 2
    plain, turned = ((1,), (0,)), ((1,), (1,))
    corner = inverse_of(normal_ref[:half, :half])
    below = normal_ref[half:, :half]
    weight = exact_dot(below, corner, plain)
    rest = inverse_of(normal_ref[half:, half:] - exact_dot(weight, below, turned))
    left, right = product_ref[:, :half], product_ref[:, half:]
    second = exact_dot(right - exact_dot(left, weight, turned), rest, plain)
    out_ref[:, half:] = second
    out_ref[:, :half] = exact_dot(left - exact_dot(second, below, plain), corner, plain)


def shards(names, sizes, tensor, factor_b, factor_c):
    slab_rows, mode_two, mode_three = tensor.shape
    width = factor_b.shape[1]
    b_chunks, c_chunks = sizes["ka"] * sizes["ia"], sizes["ja"] * sizes["ia"]
    ka_steps, ja_steps = len(bits_of(sizes["ka"])), len(bits_of(sizes["ja"]))
    slab = width // sizes["ia"]
    f32, bf16 = jnp.float32, jnp.bfloat16
    vmem = pl.BlockSpec(memory_space=pltpu.VMEM)
    dma = pltpu.SemaphoreType.DMA
    normal, product = pl.pallas_call(
        functools.partial(exchange_kernel, names, sizes),
        out_shape=(
            jax.ShapeDtypeStruct((width, width), f32),
            jax.ShapeDtypeStruct((slab_rows, width), f32),
        ),
        in_specs=[pl.BlockSpec(memory_space=pl.ANY), vmem, vmem],
        out_specs=(vmem, vmem),
        scratch_shapes=[
            pltpu.VMEM(tensor.shape, f32),
            pltpu.VMEM((b_chunks,) + factor_b.shape, f32),
            pltpu.VMEM((c_chunks,) + factor_c.shape, f32),
            pltpu.VMEM((sizes["ia"], slab, width), f32),
            pltpu.VMEM((width, width), f32),
            pltpu.VMEM((width, width), f32),
            pltpu.VMEM((ja_steps, slab, width), f32),
            pltpu.VMEM((ka_steps, slab, width), f32),
            pltpu.VMEM((ja_steps + ka_steps, slab_rows, width), f32),
            pltpu.VMEM((mode_three, width), bf16),
            pltpu.VMEM((mode_three, width), bf16),
            pltpu.VMEM((mode_two, width), f32),
            pltpu.VMEM((slab_rows, width), f32),
            dma((slab_rows,)),
            dma((b_chunks,)),
            dma((b_chunks,)),
            dma((c_chunks,)),
            dma((c_chunks,)),
            dma((sizes["ia"],)),
            dma((sizes["ia"],)),
            dma((2, ja_steps)),
            dma((2, ka_steps)),
            dma((2, ja_steps + ka_steps)),
        ],
        compiler_params=pltpu.CompilerParams(
            collective_id=0, has_side_effects=True, vmem_limit_bytes=40 * 2**20
        ),
        name="exchange",
    )(tensor, factor_b, factor_c)
    return pl.pallas_call(
        solve_kernel,
        out_shape=jax.ShapeDtypeStruct((slab_rows, width), f32),
        in_specs=[vmem, vmem],
        out_specs=vmem,
        compiler_params=pltpu.CompilerParams(vmem_limit_bytes=16 * 2**20),
        name="solve",
    )(normal, product)


def solution(mesh):
    names = tuple(mesh.axis_names)
    sizes = {name: mesh.shape[name] for name in names}
    return jax.shard_map(
        functools.partial(shards, names, sizes),
        mesh=mesh,
        in_specs=(P("ia", "ja", "ka"), P(("ja", "ka", "ia"), None), P(("ka", "ja", "ia"), None)),
        out_specs=P("ia", None),
        check_vma=False,
    )
```

time: 297 us -> 56 us (0.19); the launches traced: 291 us -> 55.7 us
  other arithmetic: 126 us -> 0 us
  blocking collectives: 68.3 us -> 0 us
  waiting for transfers between devices: 51.8 us -> 0 us
  Pallas kernels: 0 us -> 49.5 us
  matrix products: 20.8 us -> 0 us
  between operations: 17.8 us -> 0.01 us
    another operation x24 -> x0, other arithmetic: 124 us -> none  [the longest x7 34.9 us: shards(): lower_factor = jnp.linalg.cholesky(normal)]
    psum x1 -> x0, waiting for transfers between devices: 51.8 us -> none  [shards(): lax.psum((gram_of(factor_b), gram_of(factor_c)), ('ja', 'ka', 'ia'))]
    pallas_call x0 -> x2, Pallas kernels: none -> 49.5 us  [the longest x1 39.7 us: shards(): pl.pallas_call(functools.partial(exchange_kernel, names, sizes), out_shap...]
    all_gather x2 -> x0, blocking collectives: 34.9 us -> none  [the longest x1 25.1 us: shards(): lax.all_gather(factor_b, ('ka', 'ia'), axis=0, tiled=True)[None, :, :]]
    psum x1 -> x0, blocking collectives: 33.4 us -> none  [shards(): product = lax.psum(partial_sum, ('ja', 'ka'))]
    dot_general x5 -> x0, matrix products: 18.1 us -> none  [the longest x1 13.2 us: shards(): jnp.dot(unfolded, lax.all_gather(factor_c, ('ja', 'ia'), axis=0, tiled=Tr...]
    unnamed x0 -> x6, local copies, waits for them, and re-layouts: none -> 6.17 us
    another operation x13 -> x0, local copies, waits for them, and re-layouts: 4.17 us -> none
  transfers between devices with their start and end apart: 1 -> 0, of which waited for: 1 -> 0; matrix products, arithmetic and copies ran while one was open for 5% -> 0% of each run, Pallas kernels for 0% -> 0%
where the time goes in v1:
time: 56 us; the launch traced here: 55.7 us
  Pallas kernels  49.5 us (88%)
  local copies, waits for them, and re-layouts  6.17 us (11%)
    pallas_call x1, Pallas kernels, shards(): pl.pallas_call(functools.partial(exchange_kernel, names, sizes), out_shap...  39.7 us
    pallas_call x1, Pallas kernels, shards(): pl.pallas_call(solve_kernel, out_shape=jax.ShapeDtypeStruct((slab_rows, w...  9.78 us
    unnamed x6, local copies, waits for them, and re-layouts  6.17 us

profile of v1, /device:TPU:0, one launch (start us, length us, event | category | flops | bytes accessed | tf_op | source)
XLA Modules:
  0.0 55.7 jit_solution(17225565934632378353)
XLA Ops:
  0.0 0.0 copy-start
  0.0 4.6 %copy-done = f32[12,512,512]{2,1,0:T(8,128)S(1)} copy-done((f32[12,512,512]{2,1,0:T(8,128)S(1)}, f32[12,512,512]{2,1,0:T(8,128)}, u32[]{:S(2)}) %copy-start) | copy-done | bytes 12582936
  4.6 0.0 copy-start.1
  4.6 0.8 %copy-done.1 = f32[64,256]{1,0:T(8,128)S(1)} copy-done((f32[64,256]{1,0:T(8,128)S(1)}, f32[64,256]{1,0:T(8,128)}, u32[]{:S(2)}) %copy-start.1) | copy-done | bytes 65560
  5.4 0.0 copy-start.2
  5.4 0.8 %copy-done.2 = f32[32,256]{1,0:T(8,128)S(1)} copy-done((f32[32,256]{1,0:T(8,128)S(1)}, f32[32,256]{1,0:T(8,128)}, u32[]{:S(2)}) %copy-start.2) | copy-done | bytes 32792
  6.2 39.7 %exchange.1 = (f32[256,256]{1,0:T(8,128)S(1)}, f32[12,256]{1,0:T(8,128)S(1)}) custom-call(f32[12,512,512]{2,1,0:T(8,128)S(1)} %copy-done, f32[32,256]{1,0:T(8,128)S(1)} %copy-done.2, f32[64,256]{1,0:T(8,128)S(1)} %copy-done.1), custom_call_target="tpu_custom_call" | custom-call | tf_op jit(solution)/shard_map/exchange/pallas_call | solution.py:301
  45.9 9.8 %solve.1 = f32[12,256]{1,0:T(8,128)} custom-call(f32[256,256]{1,0:T(8,128)S(1)} %get-tuple-element.7.normal_ref, f32[12,256]{1,0:T(8,128)S(1)} %get-tuple-element.8.product_ref), custom_call_target="tpu_custom_call" | custom-call | tf_op jit(solution)/shard_map/solve/pallas_call | solution.py:339
Async XLA Ops:
  0.0 4.6 %copy-start = (f32[12,512,512]{2,1,0:T(8,128)S(1)}, f32[12,512,512]{2,1,0:T(8,128)}, u32[]{:S(2)}) copy-start(f32[12,512,512]{2,1,0:T(8,128)} %tensor_ref.1) | copy-start | bytes 37748740
  4.6 0.8 %copy-start.1 = (f32[64,256]{1,0:T(8,128)S(1)}, f32[64,256]{1,0:T(8,128)}, u32[]{:S(2)}) copy-start(f32[64,256]{1,0:T(8,128)} %c_ref.1) | copy-start | bytes 196612
  5.4 0.8 %copy-start.2 = (f32[32,256]{1,0:T(8,128)S(1)}, f32[32,256]{1,0:T(8,128)}, u32[]{:S(2)}) copy-start(f32[32,256]{1,0:T(8,128)} %b_ref.1) | copy-start | bytes 98308

commit v2 on v1

--- a/solution.py
+++ b/solution.py
@@ -99,8 +99,7 @@
     b_in,
     c_in,
     p_in,
-    c_high,
-    c_low,
+    c_split,
     b_flat,
     p_buf,
     t_sem,
@@ -113,6 +112,7 @@
     gb_sem,
     gc_sem,
     p_sem,
+    own_sem,
 ):
     slab_rows = tensor_ref.shape[0]
     width = b_ref.shape[1]
@@ -123,9 +123,6 @@
 
     def fetch(i):
         return pltpu.make_async_copy(tensor_ref.at[i], t_buf.at[i], t_sem.at[i])
-
-    for i in range(slab_rows):
-        fetch(i).start()
 
     partners = [partner(n, bit) for n in names for bit in bits_of(sizes[n])]
     barrier = pltpu.get_barrier_semaphore()
@@ -137,23 +134,32 @@
     b_links = [(bit * sizes["ia"], partner("ka", bit)) for bit in bits_of(sizes["ka"])] + ia_links
     c_at = at["ja"] * sizes["ia"] + at["ia"]
     b_at = at["ka"] * sizes["ia"] + at["ia"]
-    c_buf[c_at] = c_ref[...]
-    b_buf[b_at] = b_ref[...]
+    own_c = pltpu.make_async_copy(c_ref, c_buf.at[c_at], own_sem.at[0])
+    own_b = pltpu.make_async_copy(b_ref, b_buf.at[b_at], own_sem.at[1])
+    own_c.start()
+    own_b.start()
+    for i in range(slab_rows):
+        fetch(i).start()
+    own_c.wait()
+    own_b.wait()
     pl.semaphore_wait(barrier, len(partners))
 
     c_all = Gather(c_buf, c_send, c_recv, c_at, c_links)
     b_all = Gather(b_buf, b_send, b_recv, b_at, b_links)
     c_all.forward(0)
     b_all.forward(0)
-    for mask in c_all.masks():
-        c_all.arrive(mask)
-        c_all.forward(mask)
+    arrivals = [(bin(m).count("1"), 0, k, c_all, m) for k, m in enumerate(c_all.masks())]
+    arrivals += [(bin(m).count("1"), 1, k, b_all, m) for k, m in enumerate(b_all.masks())]
+    for _, _, _, gather, mask in sorted(arrivals, key=lambda a: a[:3]):
+        gather.arrive(mask)
+        gather.forward(mask)
 
     deep = c_buf.shape[0] * c_buf.shape[1]
     whole_c = c_buf[...].reshape(deep, width)
     high = whole_c.astype(jnp.bfloat16)
-    c_high[...] = high
-    c_low[...] = (whole_c - high.astype(jnp.float32)).astype(jnp.bfloat16)
+    c_split[:deep] = high
+    c_split[deep : 2 * deep] = (whole_c - high.astype(jnp.float32)).astype(jnp.bfloat16)
+    c_split[2 * deep :] = high
     gram_c[...] = exact_dot(whole_c, whole_c, ((0,), (0,)))
 
     slab = width // sizes["ia"]
@@ -175,9 +181,6 @@
     b_steps = [stage(gram_b.at[rows], b_in, gb_sem, s, d) for s, d in enumerate(ja_partners)]
     c_steps[0].start()
 
-    for mask in b_all.masks():
-        b_all.arrive(mask)
-        b_all.forward(mask)
     whole_b = b_buf[...].reshape(b_buf.shape[0] * b_buf.shape[1], width)
     b_flat[...] = whole_b
     gram_b[...] = exact_dot(whole_b, whole_b, ((0,), (0,)))
@@ -189,17 +192,10 @@
             block = t_buf[i]
             block_high = block.astype(jnp.bfloat16)
             block_low = (block - block_high.astype(jnp.float32)).astype(jnp.bfloat16)
-            dims = ((1,), (0,))
-
-            def pass_of(left, right):
-                return lax.dot_general(
-                    left, right, (dims, ((), ())), preferred_element_type=jnp.float32
-                )
-
-            section = (
-                pass_of(block_low, c_high[...])
-                + pass_of(block_high, c_low[...])
-                + pass_of(block_high, c_high[...])
+            section = jnp.dot(
+                jnp.concatenate([block_low, block_high, block_high], axis=1),
+                c_split[...],
+                preferred_element_type=jnp.float32,
             )
             p_buf[pl.ds(i, 1), :] = jnp.sum(section * b_flat[...], axis=0, keepdims=True)
             return carry
@@ -207,7 +203,8 @@
         lax.fori_loop(first, last, one, 0)
 
     pending = [("c", s) for s in range(len(c_steps))] + [("b", s) for s in range(len(b_steps))]
-    parts = len(pending) + 1
+    pending.sort(key=lambda p: p[1])
+    parts = len(pending)
     cuts = [slab_rows * p // parts for p in range(parts + 1)]
     for part, (kind, step) in enumerate(pending):
         rows_of_product(cuts[part], cuts[part + 1])
@@ -222,18 +219,23 @@
     n_buf[at["ia"]] = gram_b[rows, :] * gram_c[rows, :]
     n_all = Gather(n_buf, n_send, n_recv, at["ia"], ia_links)
     n_all.forward(0)
-    rows_of_product(cuts[parts - 1], cuts[parts])
     p_steps = [stage(p_buf, p_in, p_sem, s, d) for s, d in enumerate(ja_partners + ka_partners)]
     p_steps[0].start()
-    for mask in n_all.masks():
-        n_all.arrive(mask)
-        n_all.forward(mask)
-    normal_ref[...] = n_buf[...].reshape(width, width)
+    masks = n_all.masks()
     for step, copy in enumerate(p_steps):
         copy.wait()
         p_buf[...] += p_in[step]
         if step + 1 < len(p_steps):
             p_steps[step + 1].start()
+        for mask in masks:
+            if bin(mask).count("1") == step + 1:
+                n_all.arrive(mask)
+                n_all.forward(mask)
+    for mask in masks:
+        if bin(mask).count("1") > len(p_steps):
+            n_all.arrive(mask)
+            n_all.forward(mask)
+    normal_ref[...] = n_buf[...].reshape(width, width)
     product_ref[...] = p_buf[...]
     n_all.finish()
     b_all.finish()
@@ -304,7 +306,7 @@
             jax.ShapeDtypeStruct((width, width), f32),
             jax.ShapeDtypeStruct((slab_rows, width), f32),
         ),
-        in_specs=[pl.BlockSpec(memory_space=pl.ANY), vmem, vmem],
+        in_specs=[pl.BlockSpec(memory_space=pltpu.HBM)] * 3,
         out_specs=(vmem, vmem),
         scratch_shapes=[
             pltpu.VMEM(tensor.shape, f32),
@@ -316,8 +318,7 @@
             pltpu.VMEM((ja_steps, slab, width), f32),
             pltpu.VMEM((ka_steps, slab, width), f32),
             pltpu.VMEM((ja_steps + ka_steps, slab_rows, width), f32),
-            pltpu.VMEM((mode_three, width), bf16),
-            pltpu.VMEM((mode_three, width), bf16),
+            pltpu.VMEM((3 * mode_three, width), bf16),
             pltpu.VMEM((mode_two, width), f32),
             pltpu.VMEM((slab_rows, width), f32),
             dma((slab_rows,)),
@@ -330,6 +331,7 @@
             dma((2, ja_steps)),
             dma((2, ka_steps)),
             dma((2, ja_steps + ka_steps)),
+            dma((2,)),
         ],
         compiler_params=pltpu.CompilerParams(
             collective_id=0, has_side_effects=True, vmem_limit_bytes=40 * 2**20

time: 56 us -> 51.2 us (0.914)
  Pallas kernels: 49.5 us -> 44.7 us
    pallas_call x1, Pallas kernels: 39.7 us -> 34.9 us  [shards(): pl.pallas_call(functools.partial(exchange_kernel, names, sizes), out_shap...]
where the time goes in v2:
time: 51.2 us; the launch traced here: 50.9 us
  Pallas kernels  44.7 us (87%)
  local copies, waits for them, and re-layouts  6.17 us (12%)
    pallas_call x1, Pallas kernels, shards(): pl.pallas_call(functools.partial(exchange_kernel, names, sizes), out_shap...  34.9 us
    pallas_call x1, Pallas kernels, shards(): pl.pallas_call(solve_kernel, out_shape=jax.ShapeDtypeStruct((slab_rows, w...  9.78 us
    unnamed x6, local copies, waits for them, and re-layouts  6.17 us

profile of v2, /device:TPU:0, one launch (start us, length us, event | category | flops | bytes accessed | tf_op | source)
XLA Modules:
  0.0 50.9 jit_solution(709173542962395514)
XLA Ops:
  0.0 0.0 copy-start
  0.0 4.6 %copy-done = f32[12,512,512]{2,1,0:T(8,128)S(1)} copy-done((f32[12,512,512]{2,1,0:T(8,128)S(1)}, f32[12,512,512]{2,1,0:T(8,128)}, u32[]{:S(2)}) %copy-start) | copy-done | bytes 12582936
  4.6 0.0 copy-start.1
  4.6 0.8 %copy-done.1 = f32[64,256]{1,0:T(8,128)S(1)} copy-done((f32[64,256]{1,0:T(8,128)S(1)}, f32[64,256]{1,0:T(8,128)}, u32[]{:S(2)}) %copy-start.1) | copy-done | bytes 65560
  5.4 0.0 copy-start.2
  5.4 0.8 %copy-done.2 = f32[32,256]{1,0:T(8,128)S(1)} copy-done((f32[32,256]{1,0:T(8,128)S(1)}, f32[32,256]{1,0:T(8,128)}, u32[]{:S(2)}) %copy-start.2) | copy-done | bytes 32792
  6.2 34.9 %exchange.1 = (f32[256,256]{1,0:T(8,128)S(1)}, f32[12,256]{1,0:T(8,128)S(1)}) custom-call(f32[12,512,512]{2,1,0:T(8,128)S(1)} %copy-done, f32[32,256]{1,0:T(8,128)S(1)} %copy-done.2, f32[64,256]{1,0:T(8,128)S(1)} %copy-done.1), custom_call_target="tpu_custom_call" | custom-call | tf_op jit(solution)/shard_map/exchange/pallas_call | solution.py:303
  41.1 9.8 %solve.1 = f32[12,256]{1,0:T(8,128)} custom-call(f32[256,256]{1,0:T(8,128)S(1)} %get-tuple-element.7.normal_ref, f32[12,256]{1,0:T(8,128)S(1)} %get-tuple-element.8.product_ref), custom_call_target="tpu_custom_call" | custom-call | tf_op jit(solution)/shard_map/solve/pallas_call | solution.py:341
Async XLA Ops:
  0.0 4.6 %copy-start = (f32[12,512,512]{2,1,0:T(8,128)S(1)}, f32[12,512,512]{2,1,0:T(8,128)}, u32[]{:S(2)}) copy-start(f32[12,512,512]{2,1,0:T(8,128)} %tensor_ref.1) | copy-start | bytes 37748740
  4.6 0.8 %copy-start.1 = (f32[64,256]{1,0:T(8,128)S(1)}, f32[64,256]{1,0:T(8,128)}, u32[]{:S(2)}) copy-start(f32[64,256]{1,0:T(8,128)} %c_ref.1) | copy-start | bytes 196612
  5.4 0.8 %copy-start.2 = (f32[32,256]{1,0:T(8,128)S(1)}, f32[32,256]{1,0:T(8,128)}, u32[]{:S(2)}) copy-start(f32[32,256]{1,0:T(8,128)} %b_ref.1) | copy-start | bytes 98308

commit v3 on v2

--- a/solution.py
+++ b/solution.py
@@ -9,6 +9,7 @@
 
 exact_mode = lax.Precision.HIGHEST
 tile_rows = 8
+direct_ja, direct_ka, direct_ia, direct_n, direct_sums = True, True, False, True, True
 
 
 def bits_of(count):
@@ -38,48 +39,103 @@
     )
 
 
+def combinations_of(bits):
+    found = [0]
+    for bit in bits:
+        found += [mask | bit for mask in found]
+    return found[1:]
+
+
 class Gather:
-    def __init__(self, buffer, send_sems, recv_sems, position, links):
+    def __init__(self, buffer, send_sems, recv_sems, position, levels):
         self.buffer, self.send_sems, self.recv_sems = buffer, send_sems, recv_sems
-        self.position, self.links = position, links
+        self.position, self.levels = position, levels
         self.sends = []
-
-    def forward(self, mask):
-        low = mask & -mask
+        self.order = [(0, -1, 0)]
+        for number, level in enumerate(levels):
+            self.order += [
+                (depth + 1, number, mask | step)
+                for depth, _, mask in self.order
+                for step in level
+            ]
+        self.order = sorted(self.order[1:], key=lambda entry: entry[:2])
+
+    def copy(self, mask, arrival, device):
         chunk = flip_mask(self.position, mask)
-        for bit, device in self.links:
-            if mask == 0 or bit < low:
-                copy = pltpu.make_async_remote_copy(
-                    src_ref=self.buffer.at[chunk],
-                    dst_ref=self.buffer.at[chunk],
-                    send_sem=self.send_sems.at[mask | bit],
-                    recv_sem=self.recv_sems.at[mask | bit],
-                    device_id=device,
-                    device_id_type=pl.DeviceIdType.MESH,
-                )
-                copy.start()
-                self.sends.append(copy)
-
-    def arrive(self, mask):
-        low = mask & -mask
-        chunk = flip_mask(self.position, mask)
-        device = [d for bit, d in self.links if bit == low][0]
-        pltpu.make_async_remote_copy(
+        return pltpu.make_async_remote_copy(
             src_ref=self.buffer.at[chunk],
             dst_ref=self.buffer.at[chunk],
-            send_sem=self.send_sems.at[mask],
-            recv_sem=self.recv_sems.at[mask],
+            send_sem=self.send_sems.at[arrival],
+            recv_sem=self.recv_sems.at[arrival],
             device_id=device,
             device_id_type=pl.DeviceIdType.MESH,
-        ).wait_recv()
-
-    def masks(self):
-        count = 2 ** len(self.links)
-        return sorted(range(1, count), key=lambda m: (bin(m).count("1"), -m))
+        )
+
+    def forward(self, mask, after=-1):
+        for level in self.levels[after + 1 :]:
+            for step, device in level.items():
+                self.sends.append(self.copy(mask, mask | step, device))
+                self.sends[-1].start()
+
+    def arrive(self, mask, number):
+        level = self.levels[number]
+        step = [step for step in level if mask & sum_bits(level) == step][0]
+        self.copy(mask, mask, level[step]).wait_recv()
+        self.forward(mask, number)
 
     def finish(self):
         for copy in self.sends:
             copy.wait_send()
+
+
+def sum_bits(level):
+    union = 0
+    for step in level:
+        union |= step
+    return union
+
+
+class Total:
+    def __init__(self, buffer, inbox, sems, position, levels):
+        self.buffer, self.inbox, self.sems, self.position = buffer, inbox, sems, position
+        self.levels, self.level, self.copies = levels, 0, []
+
+    def start(self):
+        self.copies = [
+            pltpu.make_async_remote_copy(
+                src_ref=self.buffer,
+                dst_ref=self.inbox.at[step],
+                send_sem=self.sems.at[0, step],
+                recv_sem=self.sems.at[1, step],
+                device_id=device,
+                device_id_type=pl.DeviceIdType.MESH,
+            )
+            for step, device in self.levels[self.level].items()
+        ]
+        for copy in self.copies:
+            copy.start()
+
+    def advance(self):
+        if self.level == len(self.levels):
+            return
+        for copy in self.copies:
+            copy.wait()
+        terms = {0: self.buffer[...]}
+        terms.update({step: self.inbox[step] for step in self.levels[self.level]})
+        while len(terms) > 1:
+            bit = highest_bit(max(terms))
+            terms = {mask: terms[mask] + terms[mask | bit] for mask in terms if not mask & bit}
+        self.buffer[...] = terms[0]
+        self.level += 1
+        if self.level < len(self.levels):
+            self.start()
+
+
+def highest_bit(number):
+    bit = 1
+    while bit * 2 <= number:
+        bit *= 2
+    return bit
 
 
 def exchange_kernel(
@@ -98,7 +154,8 @@
     gram_c,
     b_in,
     c_in,
-    p_in,
+    pj_in,
+    pk_in,
     c_split,
     b_flat,
     p_buf,
@@ -111,27 +168,42 @@
     n_recv,
     gb_sem,
     gc_sem,
-    p_sem,
+    pj_sem,
+    pk_sem,
     own_sem,
 ):
     slab_rows = tensor_ref.shape[0]
     width = b_ref.shape[1]
     at = {name: lax.axis_index(name) for name in names}
 
-    def partner(name, bit):
-        return tuple(flip(at[n], bit) if n == name else at[n] for n in names)
+    def partner(name, mask):
+        return tuple(flip_mask(at[n], mask) if n == name else at[n] for n in names)
 
     def fetch(i):
         return pltpu.make_async_copy(tensor_ref.at[i], t_buf.at[i], t_sem.at[i])
 
-    partners = [partner(n, bit) for n in names for bit in bits_of(sizes[n])]
+    def levels_of(name, unit, direct):
+        bits = bits_of(sizes[name])
+        groups = [bits] if direct else [[bit] for bit in bits]
+        return [
+            {mask * unit: partner(name, mask) for mask in combinations_of(group)}
+            for group in groups
+        ]
+
+    ia_levels = levels_of("ia", 1, direct_ia)
+    c_levels = levels_of("ja", sizes["ia"], direct_ja) + ia_levels
+    b_levels = levels_of("ka", sizes["ia"], direct_ka) + ia_levels
+    n_levels = levels_of("ia", 1, direct_n)
+    reach = {}
+    for name in names:
+        direct = {"ia": direct_ia or direct_n, "ja": True, "ka": direct_ka or direct_sums}[name]
+        for level in levels_of(name, 1, direct):
+            reach.update({(name, mask): device for mask, device in level.items()})
+    partners = list(reach.values())
     barrier = pltpu.get_barrier_semaphore()
     for device in partners:
         pl.semaphore_signal(barrier, inc=1, device_id=device, device_id_type=pl.DeviceIdType.MESH)
 
-    ia_links = [(bit, partner("ia", bit)) for bit in bits_of(sizes["ia"])]
-    c_links = [(bit * sizes["ia"], partner("ja", bit)) for bit in bits_of(sizes["ja"])] + ia_links
-    b_links = [(bit * sizes["ia"], partner("ka", bit)) for bit in bits_of(sizes["ka"])] + ia_links
     c_at = at["ja"] * sizes["ia"] + at["ia"]
     b_at = at["ka"] * sizes["ia"] + at["ia"]
     own_c = pltpu.make_async_copy(c_ref, c_buf.at[c_at], own_sem.at[0])
@@ -144,15 +216,13 @@
     own_b.wait()
     pl.semaphore_wait(barrier, len(partners))
 
-    c_all = Gather(c_buf, c_send, c_recv, c_at, c_links)
-    b_all = Gather(b_buf, b_send, b_recv, b_at, b_links)
+    c_all = Gather(c_buf, c_send, c_recv, c_at, c_levels)
+    b_all = Gather(b_buf, b_send, b_recv, b_at, b_levels)
     c_all.forward(0)
     b_all.forward(0)
-    arrivals = [(bin(m).count("1"), 0, k, c_all, m) for k, m in enumerate(c_all.masks())]
-    arrivals += [(bin(m).count("1"), 1, k, b_all, m) for k, m in enumerate(b_all.masks())]
-    for _, _, _, gather, mask in sorted(arrivals, key=lambda a: a[:3]):
-        gather.arrive(mask)
-        gather.forward(mask)
+    arrivals = [entry + (c_all,) for entry in c_all.order] + [entry + (b_all,) for entry in b_all.order]
+    for _, number, mask, gather in sorted(arrivals, key=lambda entry: entry[:2]):
+        gather.arrive(mask, number)
 
     deep = c_buf.shape[0] * c_buf.shape[1]
     whole_c = c_buf[...].reshape(deep, width)
@@ -165,26 +235,13 @@
     slab = width // sizes["ia"]
     rows = pl.ds(pl.multiple_of(at["ia"] * slab, slab), slab)
 
-    def stage(buffer, inbox, sems, step, device):
-        return pltpu.make_async_remote_copy(
-            src_ref=buffer,
-            dst_ref=inbox.at[step],
-            send_sem=sems.at[0, step],
-            recv_sem=sems.at[1, step],
-            device_id=device,
-            device_id_type=pl.DeviceIdType.MESH,
-        )
-
-    ka_partners = [partner("ka", bit) for bit in bits_of(sizes["ka"])]
-    ja_partners = [partner("ja", bit) for bit in bits_of(sizes["ja"])]
-    c_steps = [stage(gram_c.at[rows], c_in, gc_sem, s, d) for s, d in enumerate(ka_partners)]
-    b_steps = [stage(gram_b.at[rows], b_in, gb_sem, s, d) for s, d in enumerate(ja_partners)]
-    c_steps[0].start()
-
+    gram_sum_c = Total(gram_c.at[rows], c_in, gc_sem, at["ka"], levels_of("ka", 1, direct_sums))
+    gram_sum_b = Total(gram_b.at[rows], b_in, gb_sem, at["ja"], levels_of("ja", 1, direct_sums))
+    gram_sum_c.start()
     whole_b = b_buf[...].reshape(b_buf.shape[0] * b_buf.shape[1], width)
     b_flat[...] = whole_b
     gram_b[...] = exact_dot(whole_b, whole_b, ((0,), (0,)))
-    b_steps[0].start()
+    gram_sum_b.start()
 
     def rows_of_product(first, last):
         def one(i, carry):
@@ -202,40 +259,27 @@
 
         lax.fori_loop(first, last, one, 0)
 
-    pending = [("c", s) for s in range(len(c_steps))] + [("b", s) for s in range(len(b_steps))]
-    pending.sort(key=lambda p: p[1])
-    parts = len(pending)
+    parts = max(len(gram_sum_b.levels), len(gram_sum_c.levels))
     cuts = [slab_rows * p // parts for p in range(parts + 1)]
-    for part, (kind, step) in enumerate(pending):
+    for part in range(parts):
         rows_of_product(cuts[part], cuts[part + 1])
-        steps, buffer, inbox = (
-            (c_steps, gram_c, c_in) if kind == "c" else (b_steps, gram_b, b_in)
-        )
-        steps[step].wait()
-        buffer[rows, :] += inbox[step]
-        if step + 1 < len(steps):
-            steps[step + 1].start()
+        gram_sum_c.advance()
+        gram_sum_b.advance()
 
     n_buf[at["ia"]] = gram_b[rows, :] * gram_c[rows, :]
-    n_all = Gather(n_buf, n_send, n_recv, at["ia"], ia_links)
+    n_all = Gather(n_buf, n_send, n_recv, at["ia"], n_levels)
     n_all.forward(0)
-    p_steps = [stage(p_buf, p_in, p_sem, s, d) for s, d in enumerate(ja_partners + ka_partners)]
-    p_steps[0].start()
-    masks = n_all.masks()
-    for step, copy in enumerate(p_steps):
-        copy.wait()
-        p_buf[...] += p_in[step]
-        if step + 1 < len(p_steps):
-            p_steps[step + 1].start()
-        for mask in masks:
-            if bin(mask).count("1") == step + 1:
-                n_all.arrive(mask)
-                n_all.forward(mask)
-    for mask in masks:
-        if bin(mask).count("1") > len(p_steps):
-            n_all.arrive(mask)
-            n_all.forward(mask)
+    sum_ja = Total(p_buf, pj_in, pj_sem, at["ja"], levels_of("ja", 1, direct_sums))
+    sum_ka = Total(p_buf, pk_in, pk_sem, at["ka"], levels_of("ka", 1, direct_sums))
+    sum_ja.start()
+    while sum_ja.level < len(sum_ja.levels):
+        sum_ja.advance()
+    sum_ka.start()
+    for _, number, mask in n_all.order:
+        n_all.arrive(mask, number)
     normal_ref[...] = n_buf[...].reshape(width, width)
+    while sum_ka.level < len(sum_ka.levels):
+        sum_ka.advance()
     product_ref[...] = p_buf[...]
     n_all.finish()
     b_all.finish()
@@ -295,7 +339,6 @@
     slab_rows, mode_two, mode_three = tensor.shape
     width = factor_b.shape[1]
     b_chunks, c_chunks = sizes["ka"] * sizes["ia"], sizes["ja"] * sizes["ia"]
-    ka_steps, ja_steps = len(bits_of(sizes["ka"])), len(bits_of(sizes["ja"]))
     slab = width // sizes["ia"]
     f32, bf16 = jnp.float32, jnp.bfloat16
     vmem = pl.BlockSpec(memory_space=pltpu.VMEM)
@@ -315,9 +358,10 @@
             pltpu.VMEM((sizes["ia"], slab, width), f32),
             pltpu.VMEM((width, width), f32),
             pltpu.VMEM((width, width), f32),
-            pltpu.VMEM((ja_steps, slab, width), f32),
-            pltpu.VMEM((ka_steps, slab, width), f32),
-            pltpu.VMEM((ja_steps + ka_steps, slab_rows, width), f32),
+            pltpu.VMEM((sizes["ja"], slab, width), f32),
+            pltpu.VMEM((sizes["ka"], slab, width), f32),
+            pltpu.VMEM((sizes["ja"], slab_rows, width), f32),
+            pltpu.VMEM((sizes["ka"], slab_rows, width), f32),
             pltpu.VMEM((3 * mode_three, width), bf16),
             pltpu.VMEM((mode_two, width), f32),
             pltpu.VMEM((slab_rows, width), f32),
@@ -328,13 +372,14 @@
             dma((c_chunks,)),
             dma((sizes["ia"],)),
             dma((sizes["ia"],)),
-            dma((2, ja_steps)),
-            dma((2, ka_steps)),
-            dma((2, ja_steps + ka_steps)),
+            dma((2, sizes["ja"])),
+            dma((2, sizes["ka"])),
+            dma((2, sizes["ja"])),
+            dma((2, sizes["ka"])),
             dma((2,)),
         ],
         compiler_params=pltpu.CompilerParams(
-            collective_id=0, has_side_effects=True, vmem_limit_bytes=40 * 2**20
+            collective_id=0, has_side_effects=True, vmem_limit_bytes=62 * 2**20
         ),
         name="exchange",
     )(tensor, factor_b, factor_c)

time: 51.2 us -> 45.2 us (0.88)
  local copies, waits for them, and re-layouts: 6.17 us -> 1.66 us
  Pallas kernels: 44.7 us -> 43.3 us
    unnamed x6 -> x4, local copies, waits for them, and re-layouts: 6.17 us -> 1.66 us
    pallas_call x1, Pallas kernels: 34.9 us -> 33.6 us  [shards(): pl.pallas_call(functools.partial(exchange_kernel, names, sizes), out_shap...]
where the time goes in v3:
time: 45.2 us; the launch traced here: 45 us
  Pallas kernels  43.3 us (96%)
  local copies, waits for them, and re-layouts  1.66 us (4%)
    pallas_call x1, Pallas kernels, shards(): pl.pallas_call(functools.partial(exchange_kernel, names, sizes), out_shap...  33.6 us
    pallas_call x1, Pallas kernels, shards(): pl.pallas_call(solve_kernel, out_shape=jax.ShapeDtypeStruct((slab_rows, w...  9.78 us
    unnamed x4, local copies, waits for them, and re-layouts  1.66 us

profile of v3, /device:TPU:0, one launch (start us, length us, event | category | flops | bytes accessed | tf_op | source)
XLA Modules:
  0.0 45.0 jit_solution(585804939120301916)
XLA Ops:
  0.0 33.6 %exchange.1 = (f32[256,256]{1,0:T(8,128)}, f32[12,256]{1,0:T(8,128)}) custom-call(f32[12,512,512]{2,1,0:T(8,128)} %tensor_ref.1, f32[32,256]{1,0:T(8,128)} %b_ref.1, f32[64,256]{1,0:T(8,128)} %c_ref.1), custom_call_target="tpu_custom_call" | custom-call | tf_op jit(solution)/shard_map/exchange/pallas_call | solution.py:346
  33.6 0.0 copy-start
  33.6 0.9 %copy-done = f32[256,256]{1,0:T(8,128)S(1)} copy-done((f32[256,256]{1,0:T(8,128)S(1)}, f32[256,256]{1,0:T(8,128)}, u32[]{:S(2)}) %copy-start) | copy-done | bytes 262168
  34.5 0.0 copy-start.1
  34.5 0.7 %copy-done.1 = f32[12,256]{1,0:T(8,128)S(1)} copy-done((f32[12,256]{1,0:T(8,128)S(1)}, f32[12,256]{1,0:T(8,128)}, u32[]{:S(2)}) %copy-start.1) | copy-done | bytes 12312
  35.2 9.8 %solve.1 = f32[12,256]{1,0:T(8,128)} custom-call(f32[256,256]{1,0:T(8,128)S(1)} %copy-done, f32[12,256]{1,0:T(8,128)S(1)} %copy-done.1), custom_call_target="tpu_custom_call" | custom-call | tf_op jit(solution)/shard_map/solve/pallas_call | solution.py:386
Async XLA Ops:
  33.6 1.0 %copy-start = (f32[256,256]{1,0:T(8,128)S(1)}, f32[256,256]{1,0:T(8,128)}, u32[]{:S(2)}) copy-start(f32[256,256]{1,0:T(8,128)} %get-tuple-element.7.normal_ref) | copy-start | bytes 786436
  34.5 0.7 %copy-start.1 = (f32[12,256]{1,0:T(8,128)S(1)}, f32[12,256]{1,0:T(8,128)}, u32[]{:S(2)}) copy-start(f32[12,256]{1,0:T(8,128)} %get-tuple-element.8.product_ref) | copy-start | bytes 36868

commit v4 on v3

--- a/solution.py
+++ b/solution.py
@@ -220,7 +220,9 @@
     b_all = Gather(b_buf, b_send, b_recv, b_at, b_levels)
     c_all.forward(0)
     b_all.forward(0)
-    arrivals = [entry + (c_all,) for entry in c_all.order] + [entry + (b_all,) for entry in b_all.order]
+    late = max(depth for depth, _, _ in b_all.order)
+    arrivals = [entry + (c_all,) for entry in c_all.order]
+    arrivals += [entry + (b_all,) for entry in b_all.order if entry[0] < late]
     for _, number, mask, gather in sorted(arrivals, key=lambda entry: entry[:2]):
         gather.arrive(mask, number)
 
@@ -238,6 +240,9 @@
     gram_sum_c = Total(gram_c.at[rows], c_in, gc_sem, at["ka"], levels_of("ka", 1, direct_sums))
     gram_sum_b = Total(gram_b.at[rows], b_in, gb_sem, at["ja"], levels_of("ja", 1, direct_sums))
     gram_sum_c.start()
+    for depth, number, mask in b_all.order:
+        if depth == late:
+            b_all.arrive(mask, number)
     whole_b = b_buf[...].reshape(b_buf.shape[0] * b_buf.shape[1], width)
     b_flat[...] = whole_b
     gram_b[...] = exact_dot(whole_b, whole_b, ((0,), (0,)))

time: 45.2 us -> 44.8 us (level)
    pallas_call x1, Pallas kernels: 33.6 us -> 33.1 us  [shards(): pl.pallas_call(functools.partial(exchange_kernel, names, sizes), out_shap...]
where the time goes in v4:
time: 44.8 us; the launch traced here: 44.6 us
  Pallas kernels  42.9 us (96%)
  local copies, waits for them, and re-layouts  1.66 us (4%)
    pallas_call x1, Pallas kernels, shards(): pl.pallas_call(functools.partial(exchange_kernel, names, sizes), out_shap...  33.1 us
    pallas_call x1, Pallas kernels, shards(): pl.pallas_call(solve_kernel, out_shape=jax.ShapeDtypeStruct((slab_rows, w...  9.78 us
    unnamed x4, local copies, waits for them, and re-layouts  1.66 us

profile of v4, /device:TPU:0, one launch (start us, length us, event | category | flops | bytes accessed | tf_op | source)
XLA Modules:
  0.0 44.6 jit_solution(8947820248156262702)
XLA Ops:
  0.0 33.1 %exchange.1 = (f32[256,256]{1,0:T(8,128)}, f32[12,256]{1,0:T(8,128)}) custom-call(f32[12,512,512]{2,1,0:T(8,128)} %tensor_ref.1, f32[32,256]{1,0:T(8,128)} %b_ref.1, f32[64,256]{1,0:T(8,128)} %c_ref.1), custom_call_target="tpu_custom_call" | custom-call | tf_op jit(solution)/shard_map/exchange/pallas_call | solution.py:351
  33.1 0.0 copy-start
  33.1 0.9 %copy-done = f32[256,256]{1,0:T(8,128)S(1)} copy-done((f32[256,256]{1,0:T(8,128)S(1)}, f32[256,256]{1,0:T(8,128)}, u32[]{:S(2)}) %copy-start) | copy-done | bytes 262168
  34.1 0.0 copy-start.1
  34.1 0.7 %copy-done.1 = f32[12,256]{1,0:T(8,128)S(1)} copy-done((f32[12,256]{1,0:T(8,128)S(1)}, f32[12,256]{1,0:T(8,128)}, u32[]{:S(2)}) %copy-start.1) | copy-done | bytes 12312
  34.8 9.8 %solve.1 = f32[12,256]{1,0:T(8,128)} custom-call(f32[256,256]{1,0:T(8,128)S(1)} %copy-done, f32[12,256]{1,0:T(8,128)S(1)} %copy-done.1), custom_call_target="tpu_custom_call" | custom-call | tf_op jit(solution)/shard_map/solve/pallas_call | solution.py:391
Async XLA Ops:
  33.1 1.0 %copy-start = (f32[256,256]{1,0:T(8,128)S(1)}, f32[256,256]{1,0:T(8,128)}, u32[]{:S(2)}) copy-start(f32[256,256]{1,0:T(8,128)} %get-tuple-element.7.normal_ref) | copy-start | bytes 786436
  34.1 0.7 %copy-start.1 = (f32[12,256]{1,0:T(8,128)S(1)}, f32[12,256]{1,0:T(8,128)}, u32[]{:S(2)}) copy-start(f32[12,256]{1,0:T(8,128)} %get-tuple-element.8.product_ref) | copy-start | bytes 36868

commit v5 on v4

--- a/solution.py
+++ b/solution.py
@@ -384,7 +384,7 @@
             dma((2,)),
         ],
         compiler_params=pltpu.CompilerParams(
-            collective_id=0, has_side_effects=True, vmem_limit_bytes=62 * 2**20
+            collective_id=0, has_side_effects=True, vmem_limit_bytes=54 * 2**20
         ),
         name="exchange",
     )(tensor, factor_b, factor_c)

time: 44.8 us -> 44.8 us (level)
  no operation moved by 1% of the time
where the time goes in v5:
time: 44.8 us; the launch traced here: 44.6 us
  Pallas kernels  42.9 us (96%)
  local copies, waits for them, and re-layouts  1.66 us (4%)
    pallas_call x1, Pallas kernels, shards(): pl.pallas_call(functools.partial(exchange_kernel, names, sizes), out_shap...  33.1 us
    pallas_call x1, Pallas kernels, shards(): pl.pallas_call(solve_kernel, out_shape=jax.ShapeDtypeStruct((slab_rows, w...  9.78 us
    unnamed x4, local copies, waits for them, and re-layouts  1.66 us

profile of v5, /device:TPU:0, one launch (start us, length us, event | category | flops | bytes accessed | tf_op | source)
XLA Modules:
  0.0 44.6 jit_solution(8947820248156262702)
XLA Ops:
  0.0 33.1 %exchange.1 = (f32[256,256]{1,0:T(8,128)}, f32[12,256]{1,0:T(8,128)}) custom-call(f32[12,512,512]{2,1,0:T(8,128)} %tensor_ref.1, f32[32,256]{1,0:T(8,128)} %b_ref.1, f32[64,256]{1,0:T(8,128)} %c_ref.1), custom_call_target="tpu_custom_call" | custom-call | tf_op jit(solution)/shard_map/exchange/pallas_call | solution.py:351
  33.1 0.0 copy-start
  33.1 0.9 %copy-done = f32[256,256]{1,0:T(8,128)S(1)} copy-done((f32[256,256]{1,0:T(8,128)S(1)}, f32[256,256]{1,0:T(8,128)}, u32[]{:S(2)}) %copy-start) | copy-done | bytes 262168
  34.1 0.0 copy-start.1
  34.1 0.7 %copy-done.1 = f32[12,256]{1,0:T(8,128)S(1)} copy-done((f32[12,256]{1,0:T(8,128)S(1)}, f32[12,256]{1,0:T(8,128)}, u32[]{:S(2)}) %copy-start.1) | copy-done | bytes 12312
  34.8 9.8 %solve.1 = f32[12,256]{1,0:T(8,128)} custom-call(f32[256,256]{1,0:T(8,128)S(1)} %copy-done, f32[12,256]{1,0:T(8,128)S(1)} %copy-done.1), custom_call_target="tpu_custom_call" | custom-call | tf_op jit(solution)/shard_map/solve/pallas_call | solution.py:391
Async XLA Ops:
  33.1 1.0 %copy-start = (f32[256,256]{1,0:T(8,128)S(1)}, f32[256,256]{1,0:T(8,128)}, u32[]{:S(2)}) copy-start(f32[256,256]{1,0:T(8,128)} %get-tuple-element.7.normal_ref) | copy-start | bytes 786436
  34.1 0.7 %copy-start.1 = (f32[12,256]{1,0:T(8,128)S(1)}, f32[12,256]{1,0:T(8,128)}, u32[]{:S(2)}) copy-start(f32[12,256]{1,0:T(8,128)} %get-tuple-element.8.product_ref) | copy-start | bytes 36868
